TPU v7x, 32 devices: a whole 2x2x4 slice. The times are simulated.
32 devices in a mesh: groups: 2 (over y), tiles: 4 (over z), section: 4 (over x, core).
Axes of the slice: x: 2, y: 2, z: 4, core: 2. Of those that a mesh axis runs over, the one named last changes fastest.
Arguments:
- latents: float32 [4, 192, 8, 128], P('groups', None, 'tiles'), parts along dimension 0, may hold values from -6 to 6
- conv_weight: float32 [4, 27, 192, 192], P('section'), may hold values from -0.078125 to 0.078125
- gain: float32 [4, 192], P('section'), may hold values from 0.1 to 1.9
Outputs:
- decoded: float32 [4, 192, 8, 128], P('groups', 'section', 'tiles'), parts along dimension 0
There are 2 independent parts, one for each index of `groups`. A program takes and returns all parts, laid end to end along the dimension named above; an argument that names none is the same for every part. Nothing has to cross between parts.
All inputs are finite; a program needn't handle non-finite values.
Results may differ from a plain program's by a relative error of at most 0.00013.
Values sent between devices are 32-bit elements; how exact they have to be, the bound alone decides.
A program may use at most 64 MiB of HBM per device.

v0:
```python
import jax
import jax.numpy as jnp
from jax import lax
from jax.sharding import PartitionSpec as P

EPSILON = 1e-06


def extended(block, sides, width):
    for axis, dim in sides:
        count = lax.axis_size(axis)
        forward = [(i, i + 1) for i in range(count - 1)]
        backward = [(target, source) for source, target in forward]
        low = lax.ppermute(
            lax.slice_in_dim(block, block.shape[dim] - width, None, axis=dim), axis, forward
        )
        high = lax.ppermute(lax.slice_in_dim(block, 0, width, axis=dim), axis, backward)
        block = jnp.concatenate([low, block, high], axis=dim)
    return block


def from_behind(value, axis, by):
    peers = lax.axis_size(axis)
    pairs = [(i, i + by) for i in range(peers) if 0 <= i + by < peers]
    return lax.ppermute(value, axis, pairs)


def broadcast(value, axis, source):
    kept = jnp.where(lax.axis_index(axis) == source, value, 0).astype(value.dtype)
    return lax.psum(kept, axis)


def normalize(values, gain_row):
    meansq = jnp.mean(values * values, axis=1, keepdims=True)
    scaled = values * lax.rsqrt(meansq + EPSILON) * gain_row[None, :, None, None]
    return jax.nn.silu(scaled)


def add_rim(normed):
    return extended(normed, (("tiles", 2),), 1)


def convolve(padded, kernel, block_len, rows_here, col_count):
    summed = jnp.zeros((block_len, kernel.shape[1], rows_here, col_count), jnp.float32)
    for time_off in range(3):
        for row_off in range(3):
            for col_off in range(3):
                window = padded[
                    time_off : time_off + block_len,
                    :,
                    row_off : row_off + rows_here,
                    col_off : col_off + col_count,
                ]
                summed = summed + jnp.einsum(
                    "oi,tirw->torw",
                    kernel[time_off * 9 + row_off * 3 + col_off],
                    window,
                    precision=lax.Precision.HIGHEST,
                )
    return summed


def by_layers(latents, conv_weight, gain):
    kernel = conv_weight[0]
    gain_row = gain[0]
    frame_count, channels, rows_here, col_count = latents.shape
    layer_count = lax.axis_size("section")
    position = lax.axis_index("section")
    block_count = frame_count // frame_count
    step_count = block_count + layer_count - 1
    initial = jnp.zeros((frame_count, channels, rows_here, col_count), jnp.float32)
    memory_init = jnp.zeros((2, channels, rows_here + 2, col_count), jnp.float32)
    results_init = jnp.zeros_like(latents)

    def compute(operand):
        return convolve(operand, kernel, frame_count, rows_here, col_count)

    def skipped(operand):
        return jnp.zeros((frame_count, channels, rows_here, col_count), jnp.float32)

    def advance(step_now, loop_state):
        passing, memory, results = loop_state
        incoming = from_behind(passing, "section", 1)
        block_index = step_now - position
        active = (block_index >= 0) & (block_index < block_count)
        source = jnp.where(position == 0, latents, incoming)
        normed = normalize(source, gain_row)
        with_rim = add_rim(normed)
        joined = jnp.concatenate([memory, with_rim], axis=0)
        padded = jnp.pad(joined, ((0, 0), (0, 0), (0, 0), (1, 1)))
        branch = lax.cond(active, compute, skipped, padded)
        output = source + branch
        memory = jnp.where(active, joined[-2:], memory)
        store_now = active & (position == layer_count - 1)
        results = jnp.where(store_now, output, results)
        return (output, memory, results)

    final_state = lax.fori_loop(0, step_count, advance, (initial, memory_init, results_init))
    gathered = broadcast(final_state[2], "section", layer_count - 1)
    share = channels // layer_count
    return lax.dynamic_slice_in_dim(gathered, position * share, share, 1)


def local(latents, conv_weight, gain):
    return by_layers(latents, conv_weight, gain)


def solution(mesh):
    return jax.shard_map(
        local,
        mesh=mesh,
        in_specs=(
            P("groups", None, "tiles", None),
            P("section", None, None, None),
            P("section", None),
        ),
        out_specs=P("groups", "section", "tiles", None),
        check_vma=False,
    )
```

profile of v0, /device:TPU:0, one launch (start us, length us, event | category | flops | bytes accessed | tf_op | source)
XLA Modules:
  0.0 192.4 jit_solution(15802440383919716907)
XLA Ops:
  7.6 99.6 %while.20 = (s32[]{:T(128)}, f32[2,192,2,128]{3,1,2,0:T(8,128)S(1)}, f32[2,192,4,128]{3,1,2,0:T(8,128)S(1)}, f32[2,192,2,128]{3,1,2,0:T(8,128)S(1)}, pred[]{:T(5...) while((s32[]{:T(128)}, ...), condition=%wide.region_4.5_spmd.clone, body=%wide.region_0.4_spmd.clone.sunk | while | flops 6121095680 | bytes 99492952 | solution.py:98
  7.6 2.4 %collective-permute-start = (f32[2,192,2,128]{3,1,2,0:T(8,128)S(1)}, f32[2,192,2,128]{3,1,2,0:T(8,128)S(1)}, u32[]{:S(2)}, u32[]{:S(2)}) collective-permute-start(f32[2,192,2,128]{3,1,2,0:T(8,128)S(1)} %broadcast_select_fusion.6), channel_id=1, source_target_pairs={{0,1},{1,2},{2,3},{4,5},{5,6},{6,7},{8,9},{9,10},{10,11},{12,13},{... | collective-permute-start | bytes 1179656 | tf_op jit(solution)/shard_map/while/body/eval_jaxpr/ppermute | solution.py:25
  10.0 1.3 collective-permute-done
  12.3 1.3 collective-permute-start.1
  13.6 5.0 %collective-permute-start.2 = (f32[2,192,1,128]{3,1,2,0:T(8,128)S(1)}, f32[2,192,1,128]{3,1,2,0:T(8,128)S(1)}, u32[]{:S(2)}, u32[]{:S(2)}) collective-permute-start(f32[2,192,1,128]{3,1,2,0:T(8,128)S(1)} %get-tuple-element.376), channel_id=1, source_target_pairs={{0,4},{4,8},{8,12},{1,5},{5,9},{9,13},{2,6},{6,10},{10,14},{3,7},{... | collective-permute-start | bytes 589832 | tf_op jit(solution)/shard_map/while/body/eval_jaxpr/ppermute | solution.py:14
  18.6 1.7 collective-permute-done.1
  20.2 1.5 collective-permute-done.2
  22.1 19.5 %conditional.3 = (f32[2,192,2,128]{3,1,2,0:T(8,128)S(1)}) conditional(s32[]{:T(128)} %convert_element_type.22, () %tuple.63, (f32[4,192,4,128]{3,1,2,0:T(8,128)S(1)}, f32[27,192,192]{2,1,0:T(8,128)}) %tuple.64), branch_computations={%region_2.2_spmd, %region_3.3_spmd} | conditional | flops 6117851136 | bytes 84541480 | solution.py:91
  22.1 1.6 fusion.46
  23.7 1.6 convolution_add_fusion.10
  25.3 1.6 convolution_add_fusion.9
  41.8 1.3 collective-permute-start
  43.2 1.3 collective-permute-done
  45.4 1.3 collective-permute-start.1
  46.7 5.0 %collective-permute-start.2 = (f32[2,192,1,128]{3,1,2,0:T(8,128)S(1)}, f32[2,192,1,128]{3,1,2,0:T(8,128)S(1)}, u32[]{:S(2)}, u32[]{:S(2)}) collective-permute-start(f32[2,192,1,128]{3,1,2,0:T(8,128)S(1)} %get-tuple-element.376), channel_id=1, source_target_pairs={{0,4},{4,8},{8,12},{1,5},{5,9},{9,13},{2,6},{6,10},{10,14},{3,7},{... | collective-permute-start | bytes 589832 | tf_op jit(solution)/shard_map/while/body/eval_jaxpr/ppermute | solution.py:14
  51.8 3.5 %collective-permute-done.1 = f32[2,192,1,128]{3,1,2,0:T(8,128)S(1)} collective-permute-done((f32[2,192,1,128]{3,1,2,0:T(8,128)S(1)}, f32[2,192,1,128]{3,1,2,0:T(8,128)S(1)}, u32[]{:S(2)}, u32[]{:S(2)}) %collective-permute-start.1) | collective-permute-done | bytes 196640 | tf_op jit(solution)/shard_map/while/body/eval_jaxpr/ppermute | solution.py:17
  55.3 1.2 collective-permute-done.2
  57.1 20.9 %collective-permute-start = (f32[2,192,2,128]{3,1,2,0:T(8,128)S(1)}, f32[2,192,2,128]{3,1,2,0:T(8,128)S(1)}, u32[]{:S(2)}, u32[]{:S(2)}) collective-permute-start(f32[2,192,2,128]{3,1,2,0:T(8,128)S(1)} %broadcast_select_fusion.6), channel_id=1, source_target_pairs={{0,1},{1,2},{2,3},{4,5},{5,6},{6,7},{8,9},{9,10},{10,11},{12,13},{... | collective-permute-start | bytes 1179656 | tf_op jit(solution)/shard_map/while/body/eval_jaxpr/ppermute | solution.py:25
  78.1 1.3 collective-permute-done
  80.4 1.3 collective-permute-start.1
  81.7 5.0 %collective-permute-start.2 = (f32[2,192,1,128]{3,1,2,0:T(8,128)S(1)}, f32[2,192,1,128]{3,1,2,0:T(8,128)S(1)}, u32[]{:S(2)}, u32[]{:S(2)}) collective-permute-start(f32[2,192,1,128]{3,1,2,0:T(8,128)S(1)} %get-tuple-element.376), channel_id=1, source_target_pairs={{0,4},{4,8},{8,12},{1,5},{5,9},{9,13},{2,6},{6,10},{10,14},{3,7},{... | collective-permute-start | bytes 589832 | tf_op jit(solution)/shard_map/while/body/eval_jaxpr/ppermute | solution.py:14
  86.7 1.7 collective-permute-done.1
  88.4 1.5 collective-permute-done.2
  90.5 4.5 %collective-permute-start = (f32[2,192,2,128]{3,1,2,0:T(8,128)S(1)}, f32[2,192,2,128]{3,1,2,0:T(8,128)S(1)}, u32[]{:S(2)}, u32[]{:S(2)}) collective-permute-start(f32[2,192,2,128]{3,1,2,0:T(8,128)S(1)} %broadcast_select_fusion.6), channel_id=1, source_target_pairs={{0,1},{1,2},{2,3},{4,5},{5,6},{6,7},{8,9},{9,10},{10,11},{12,13},{... | collective-permute-start | bytes 1179656 | tf_op jit(solution)/shard_map/while/body/eval_jaxpr/ppermute | solution.py:25
  95.0 1.3 collective-permute-done
  97.3 1.3 collective-permute-start.1
  98.6 4.7 %collective-permute-start.2 = (f32[2,192,1,128]{3,1,2,0:T(8,128)S(1)}, f32[2,192,1,128]{3,1,2,0:T(8,128)S(1)}, u32[]{:S(2)}, u32[]{:S(2)}) collective-permute-start(f32[2,192,1,128]{3,1,2,0:T(8,128)S(1)} %get-tuple-element.376), channel_id=1, source_target_pairs={{0,4},{4,8},{8,12},{1,5},{5,9},{9,13},{2,6},{6,10},{10,14},{3,7},{... | collective-permute-start | bytes 589832 | tf_op jit(solution)/shard_map/while/body/eval_jaxpr/ppermute | solution.py:14
  103.3 1.7 collective-permute-done.1
  105.0 1.5 collective-permute-done.2
  107.1 1.1 copy_select_fusion
  108.3 75.7 %all-reduce.3.cloned.1.call-done = f32[2,192,2,128]{3,2,1,0:T(2,128)} async-done(((f32[2,192,2,128]{3,2,1,0:T(2,128)}), f32[2,192,2,128]{3,2,1,0:T(2,128)}) %all-reduce.3.cloned.1.call-update) | async-done | bytes 393232 | tf_op jit(solution)/shard_map/psum | solution.py:30
  184.0 1.5 constant_dynamic-slice_fusion
  (70 shorter events, 22.0 us)
Async XLA Ops:
  6.5 177.5 %all-reduce.3.cloned.1.call-start = ((), (), s32[]{:S(2)}) async-start(), calls=%async_computation | async-start | bytes 786432 | tf_op jit(solution)/shard_map/psum | solution.py:30
  7.6 3.7 %collective-permute-start = (f32[2,192,2,128]{3,1,2,0:T(8,128)S(1)}, f32[2,192,2,128]{3,1,2,0:T(8,128)S(1)}, u32[]{:S(2)}, u32[]{:S(2)}) collective-permute-start(f32[2,192,2,128]{3,1,2,0:T(8,128)S(1)} %broadcast_select_fusion.6), channel_id=1, source_target_pairs={{0,1},{1,2},{2,3},{4,5},{5,6},{6,7},{8,9},{9,10},{10,11},{12,13},{... | collective-permute-start | bytes 1179656 | tf_op jit(solution)/shard_map/while/body/eval_jaxpr/ppermute | solution.py:25
  12.3 8.0 %collective-permute-start.1 = (f32[2,192,1,128]{3,1,2,0:T(8,128)S(1)}, f32[2,192,1,128]{3,1,2,0:T(8,128)S(1)}, u32[]{:S(2)}, u32[]{:S(2)}) collective-permute-start(f32[2,192,1,128]{3,1,2,0:T(8,128)S(1)} %get-tuple-element.375), channel_id=1, source_target_pairs={{4,0},{8,4},{12,8},{5,1},{9,5},{13,9},{6,2},{10,6},{14,10},{7,3},{... | collective-permute-start | bytes 589832 | tf_op jit(solution)/shard_map/while/body/eval_jaxpr/ppermute | solution.py:17
  13.6 8.1 %collective-permute-start.2 = (f32[2,192,1,128]{3,1,2,0:T(8,128)S(1)}, f32[2,192,1,128]{3,1,2,0:T(8,128)S(1)}, u32[]{:S(2)}, u32[]{:S(2)}) collective-permute-start(f32[2,192,1,128]{3,1,2,0:T(8,128)S(1)} %get-tuple-element.376), channel_id=1, source_target_pairs={{0,4},{4,8},{8,12},{1,5},{5,9},{9,13},{2,6},{6,10},{10,14},{3,7},{... | collective-permute-start | bytes 589832 | tf_op jit(solution)/shard_map/while/body/eval_jaxpr/ppermute | solution.py:14
  22.1 4.8 %copy-start = (f32[27,192,192]{2,1,0:T(8,128)S(1)}, f32[27,192,192]{2,1,0:T(8,128)}, u32[]{:S(2)}) copy-start(f32[27,192,192]{2,1,0:T(8,128)} %get-tuple-element.219) | copy-start | bytes 11943940 | tf_op jit(solution)/shard_map/while/body/eval_jaxpr/cond
  41.8 2.6 %collective-permute-start = (f32[2,192,2,128]{3,1,2,0:T(8,128)S(1)}, f32[2,192,2,128]{3,1,2,0:T(8,128)S(1)}, u32[]{:S(2)}, u32[]{:S(2)}) collective-permute-start(f32[2,192,2,128]{3,1,2,0:T(8,128)S(1)} %broadcast_select_fusion.6), channel_id=1, source_target_pairs={{0,1},{1,2},{2,3},{4,5},{5,6},{6,7},{8,9},{9,10},{10,11},{12,13},{... | collective-permute-start | bytes 1179656 | tf_op jit(solution)/shard_map/while/body/eval_jaxpr/ppermute | solution.py:25
  45.4 9.8 %collective-permute-start.1 = (f32[2,192,1,128]{3,1,2,0:T(8,128)S(1)}, f32[2,192,1,128]{3,1,2,0:T(8,128)S(1)}, u32[]{:S(2)}, u32[]{:S(2)}) collective-permute-start(f32[2,192,1,128]{3,1,2,0:T(8,128)S(1)} %get-tuple-element.375), channel_id=1, source_target_pairs={{4,0},{8,4},{12,8},{5,1},{9,5},{13,9},{6,2},{10,6},{14,10},{7,3},{... | collective-permute-start | bytes 589832 | tf_op jit(solution)/shard_map/while/body/eval_jaxpr/ppermute | solution.py:17
  46.7 9.7 %collective-permute-start.2 = (f32[2,192,1,128]{3,1,2,0:T(8,128)S(1)}, f32[2,192,1,128]{3,1,2,0:T(8,128)S(1)}, u32[]{:S(2)}, u32[]{:S(2)}) collective-permute-start(f32[2,192,1,128]{3,1,2,0:T(8,128)S(1)} %get-tuple-element.376), channel_id=1, source_target_pairs={{0,4},{4,8},{8,12},{1,5},{5,9},{9,13},{2,6},{6,10},{10,14},{3,7},{... | collective-permute-start | bytes 589832 | tf_op jit(solution)/shard_map/while/body/eval_jaxpr/ppermute | solution.py:14
  57.1 22.2 %collective-permute-start = (f32[2,192,2,128]{3,1,2,0:T(8,128)S(1)}, f32[2,192,2,128]{3,1,2,0:T(8,128)S(1)}, u32[]{:S(2)}, u32[]{:S(2)}) collective-permute-start(f32[2,192,2,128]{3,1,2,0:T(8,128)S(1)} %broadcast_select_fusion.6), channel_id=1, source_target_pairs={{0,1},{1,2},{2,3},{4,5},{5,6},{6,7},{8,9},{9,10},{10,11},{12,13},{... | collective-permute-start | bytes 1179656 | tf_op jit(solution)/shard_map/while/body/eval_jaxpr/ppermute | solution.py:25
  80.4 8.0 %collective-permute-start.1 = (f32[2,192,1,128]{3,1,2,0:T(8,128)S(1)}, f32[2,192,1,128]{3,1,2,0:T(8,128)S(1)}, u32[]{:S(2)}, u32[]{:S(2)}) collective-permute-start(f32[2,192,1,128]{3,1,2,0:T(8,128)S(1)} %get-tuple-element.375), channel_id=1, source_target_pairs={{4,0},{8,4},{12,8},{5,1},{9,5},{13,9},{6,2},{10,6},{14,10},{7,3},{... | collective-permute-start | bytes 589832 | tf_op jit(solution)/shard_map/while/body/eval_jaxpr/ppermute | solution.py:17
  81.7 8.2 %collective-permute-start.2 = (f32[2,192,1,128]{3,1,2,0:T(8,128)S(1)}, f32[2,192,1,128]{3,1,2,0:T(8,128)S(1)}, u32[]{:S(2)}, u32[]{:S(2)}) collective-permute-start(f32[2,192,1,128]{3,1,2,0:T(8,128)S(1)} %get-tuple-element.376), channel_id=1, source_target_pairs={{0,4},{4,8},{8,12},{1,5},{5,9},{9,13},{2,6},{6,10},{10,14},{3,7},{... | collective-permute-start | bytes 589832 | tf_op jit(solution)/shard_map/while/body/eval_jaxpr/ppermute | solution.py:14
  90.5 5.8 %collective-permute-start = (f32[2,192,2,128]{3,1,2,0:T(8,128)S(1)}, f32[2,192,2,128]{3,1,2,0:T(8,128)S(1)}, u32[]{:S(2)}, u32[]{:S(2)}) collective-permute-start(f32[2,192,2,128]{3,1,2,0:T(8,128)S(1)} %broadcast_select_fusion.6), channel_id=1, source_target_pairs={{0,1},{1,2},{2,3},{4,5},{5,6},{6,7},{8,9},{9,10},{10,11},{12,13},{... | collective-permute-start | bytes 1179656 | tf_op jit(solution)/shard_map/while/body/eval_jaxpr/ppermute | solution.py:25
  97.3 7.7 %collective-permute-start.1 = (f32[2,192,1,128]{3,1,2,0:T(8,128)S(1)}, f32[2,192,1,128]{3,1,2,0:T(8,128)S(1)}, u32[]{:S(2)}, u32[]{:S(2)}) collective-permute-start(f32[2,192,1,128]{3,1,2,0:T(8,128)S(1)} %get-tuple-element.375), channel_id=1, source_target_pairs={{4,0},{8,4},{12,8},{5,1},{9,5},{13,9},{6,2},{10,6},{14,10},{7,3},{... | collective-permute-start | bytes 589832 | tf_op jit(solution)/shard_map/while/body/eval_jaxpr/ppermute | solution.py:17
  98.6 7.9 %collective-permute-start.2 = (f32[2,192,1,128]{3,1,2,0:T(8,128)S(1)}, f32[2,192,1,128]{3,1,2,0:T(8,128)S(1)}, u32[]{:S(2)}, u32[]{:S(2)}) collective-permute-start(f32[2,192,1,128]{3,1,2,0:T(8,128)S(1)} %get-tuple-element.376), channel_id=1, source_target_pairs={{0,4},{4,8},{8,12},{1,5},{5,9},{9,13},{2,6},{6,10},{10,14},{3,7},{... | collective-permute-start | bytes 589832 | tf_op jit(solution)/shard_map/while/body/eval_jaxpr/ppermute | solution.py:14
Sparse Core Ops, SparseCore 0:
  108.4 75.5 all-reduce.2
where the time goes:
time: 193 us; the launch traced here: 192 us
  waiting for transfers between devices  95.1 us (49%)
  starting transfers between devices  54 us (28%)
  matrix products  19.2 us (10%)
  between operations  13.4 us (7%)
  other arithmetic  7.2 us (4%)
  local copies, waits for them, and re-layouts  2.76 us (1%)
    psum x1, waiting for transfers between devices, broadcast(): return lax.psum(kept, axis)  75.7 us
    ppermute x4, starting transfers between devices, from_behind(): return lax.ppermute(value, axis, pairs)  29.1 us
    ppermute x4, starting transfers between devices, extended(): lax.ppermute(lax.slice_in_dim(block, block.shape[dim] - width, None, axis...  19.7 us
    dot_general x27, matrix products, convolve(): jnp.einsum('oi,tirw->torw', kernel[time_off * 9 + row_off * 3 + col_off],...  19.2 us
    ppermute x4, waiting for transfers between devices, extended(): lax.ppermute(lax.slice_in_dim(block, 0, width, axis=dim), axis, backward)  8.51 us
    ppermute x4, waiting for transfers between devices, extended(): lax.ppermute(lax.slice_in_dim(block, block.shape[dim] - width, None, axis...  5.56 us
    ppermute x4, waiting for transfers between devices, from_behind(): return lax.ppermute(value, axis, pairs)  5.23 us
    ppermute x4, starting transfers between devices, extended(): lax.ppermute(lax.slice_in_dim(block, 0, width, axis=dim), axis, backward)  5.17 us
  transfers between devices with their start and end apart: 13, of which 13 were waited for; matrix products, arithmetic and copies ran while one was open for 0% of the time, Pallas kernels for 0%

commit v1 on v0

v1 whole, which is shorter than its diff:
```python
import functools

import jax
import jax.numpy as jnp
from jax import lax
from jax.experimental import pallas as pl
from jax.experimental.pallas import tpu as pltpu
from jax.sharding import PartitionSpec as P

EPSILON = 1e-06
MESH = pl.DeviceIdType.MESH


def halves(value):
    high = value.astype(jnp.bfloat16)
    low = (value - high.astype(jnp.float32)).astype(jnp.bfloat16)
    return high, low


def kernel(
    dims,
    lat_ref, weight_ref, gain_ref, out_ref,
    raw, w_high, w_low, main, halo, n_high, n_low, acc, result, stage, gain_col,
    weight_sem, main_send, main_recv, halo_send, halo_recv, out_send, out_recv, own_sem,
):
    frames, rows, channels, cols, layers, tiles, first_tap = dims
    share = channels // layers
    section = lax.axis_index("section")
    tile = lax.axis_index("tiles")
    last = layers - 1
    has_up = tile > 0
    has_down = tile < tiles - 1
    taps = 3 - first_tap

    def weight_copy(a, b):
        return pltpu.make_async_copy(
            weight_ref.at[0, pl.ds(9 * (a + first_tap) + 3 * b, 3)],
            raw.at[a, b],
            weight_sem.at[a, b],
        )

    order = [(a, b) for a in reversed(range(taps)) for b in (1, 0, 2)]
    for a, b in order:
        weight_copy(a, b).start()

    barrier = pltpu.get_barrier_semaphore()

    def greet(condition, target):
        @pl.when(condition)
        def _():
            pl.semaphore_signal(barrier, inc=1, device_id=target, device_id_type=MESH)

    links = [
        (has_up, {"tiles": tile - 1}),
        (has_down, {"tiles": tile + 1}),
        (section > 0, {"section": section - 1}),
        (section < last, {"section": section + 1}),
        (section < last, {"section": last}),
    ]
    links += [(section == last, {"section": peer}) for peer in range(last)]
    for condition, target in links:
        greet(condition, target)

    def up_copy(f):
        return pltpu.make_async_remote_copy(
            src_ref=main.at[f, 0], dst_ref=halo.at[f, 1],
            send_sem=halo_send.at[f, 0], recv_sem=halo_recv.at[f, 1],
            device_id={"tiles": tile - 1}, device_id_type=MESH,
        )

    def down_copy(f):
        return pltpu.make_async_remote_copy(
            src_ref=main.at[f, rows - 1], dst_ref=halo.at[f, 0],
            send_sem=halo_send.at[f, 1], recv_sem=halo_recv.at[f, 0],
            device_id={"tiles": tile + 1}, device_id_type=MESH,
        )

    def main_copy(f):
        return pltpu.make_async_remote_copy(
            src_ref=result.at[f], dst_ref=main.at[f],
            send_sem=main_send.at[f], recv_sem=main_recv.at[f],
            device_id={"section": section + 1}, device_id_type=MESH,
        )

    def out_copy(f, peer):
        return pltpu.make_async_remote_copy(
            src_ref=stage.at[f, pl.ds(peer * share * rows, share * rows)],
            dst_ref=out_ref.at[f],
            send_sem=out_send.at[f, peer], recv_sem=out_recv.at[f],
            device_id={"section": peer}, device_id_type=MESH,
        )

    def own_copy(f):
        return pltpu.make_async_copy(
            stage.at[f, pl.ds(last * share * rows, share * rows)], out_ref.at[f], own_sem.at[f]
        )

    def send_edges(f):
        @pl.when(has_up)
        def _():
            up_copy(f).start()

        @pl.when(has_down)
        def _():
            down_copy(f).start()

    @pl.when(section == 0)
    def _():
        for f in range(frames):
            for r in range(rows):
                main[f, r] = lat_ref[f, pl.ds(r, channels, stride=rows), :]

    @pl.when(jnp.logical_not(has_up))
    def _():
        for f in range(frames):
            halo[f, 0] = jnp.zeros((channels, cols), jnp.float32)

    @pl.when(jnp.logical_not(has_down))
    def _():
        for f in range(frames):
            halo[f, 1] = jnp.zeros((channels, cols), jnp.float32)

    pl.semaphore_wait(barrier, sum(condition.astype(jnp.int32) for condition, _ in links))

    @pl.when(section == 0)
    def _():
        for f in range(frames):
            send_edges(f)

    diagonal = lax.broadcasted_iota(jnp.int32, (channels, channels), 0) == (
        lax.broadcasted_iota(jnp.int32, (channels, channels), 1)
    )
    column = jnp.sum(
        jnp.where(diagonal, jnp.broadcast_to(gain_ref[0:1, :], (channels, channels)), 0.0),
        axis=1, keepdims=True,
    )
    gain_col[...] = jnp.broadcast_to(column, (channels, cols))

    for a, b in order:
        weight_copy(a, b).wait()
        for e in range(3):
            high, low = halves(raw[a, b, e])
            w_high[a, b, pl.ds(e * channels, channels), :] = high
            w_low[a, b, pl.ds(e * channels, channels), :] = low

    def normalize(values, f, place):
        meansq = jnp.mean(values * values, axis=0, keepdims=True)
        scaled = values * lax.rsqrt(meansq + EPSILON) * gain_col[...]
        high, low = halves(scaled / (1.0 + jnp.exp(-scaled)))
        n_high[f, place] = high
        n_low[f, place] = low

    def add_taps(f, a, offsets, fresh):
        source = f - 2 + a + first_tap
        total = None
        for b in offsets:
            high = jnp.concatenate([n_high[source, r + b] for r in range(rows)], axis=1)
            low = jnp.concatenate([n_low[source, r + b] for r in range(rows)], axis=1)
            part = jnp.dot(w_high[a, b], high, preferred_element_type=jnp.float32)
            part += jnp.dot(w_low[a, b], high, preferred_element_type=jnp.float32)
            part += jnp.dot(w_high[a, b], low, preferred_element_type=jnp.float32)
            total = part if total is None else total + part
        if fresh:
            acc[f] = total
        else:
            acc[f] = acc[f] + total

    lane = lax.broadcasted_iota(jnp.int32, (channels, cols), 1)

    for f in range(frames):
        fresh = True
        for a in range(taps - 1):
            if f - 2 + a + first_tap >= 0:
                add_taps(f, a, (0, 1, 2), fresh)
                fresh = False

        @pl.when(section > 0)
        def _():
            main_copy(f).wait_recv()
            send_edges(f)

        for r in range(rows):
            normalize(main[f, r], f, r + 1)
        add_taps(f, taps - 1, (1,), fresh)

        @pl.when(has_up)
        def _():
            down_copy(f).wait_recv()

        @pl.when(has_down)
        def _():
            up_copy(f).wait_recv()

        normalize(halo[f, 0], f, 0)
        normalize(halo[f, 1], f, rows + 1)
        add_taps(f, taps - 1, (0, 2), False)
        for r in range(rows):
            here = pl.ds(r * cols, cols)
            before = pltpu.roll(acc[f, pl.ds(0, channels), here], 1, 1)
            after = pltpu.roll(acc[f, pl.ds(2 * channels, channels), here], cols - 1, 1)
            result[f, r] = (
                main[f, r]
                + acc[f, pl.ds(channels, channels), here]
                + jnp.where(lane > 0, before, 0.0)
                + jnp.where(lane < cols - 1, after, 0.0)
            )

        @pl.when(section < last)
        def _():
            main_copy(f).start()

        @pl.when(section == last)
        def _():
            for r in range(rows):
                stage[f, pl.ds(r, channels, stride=rows), :] = result[f, r]
            for peer in range(last):
                out_copy(f, peer).start()
            own_copy(f).start()

    for f in range(frames):
        @pl.when(has_up)
        def _():
            up_copy(f).wait_send()

        @pl.when(has_down)
        def _():
            down_copy(f).wait_send()

        @pl.when(section < last)
        def _():
            main_copy(f).wait_send()

        @pl.when(section == last)
        def _():
            for peer in range(last):
                out_copy(f, peer).wait_send()
            own_copy(f).wait()

    @pl.when(section < last)
    def _():
        for f in range(frames):
            out_copy(f, 0).wait_recv()


def local(latents, conv_weight, gain):
    frames, channels, rows, cols = latents.shape
    layers = lax.axis_size("section")
    tiles = lax.axis_size("tiles")
    share = channels // layers
    first_tap = max(0, 3 - frames)
    taps = 3 - first_tap
    f32, bf16 = jnp.float32, jnp.bfloat16
    dma = pltpu.SemaphoreType.DMA
    macs = frames * rows * cols * channels * channels * 27
    out = pl.pallas_call(
        functools.partial(kernel, (frames, rows, channels, cols, layers, tiles, first_tap)),
        out_shape=jax.ShapeDtypeStruct((frames, share * rows, cols), f32),
        in_specs=[
            pl.BlockSpec(memory_space=pltpu.VMEM),
            pl.BlockSpec(memory_space=pltpu.HBM),
            pl.BlockSpec(memory_space=pltpu.VMEM),
        ],
        out_specs=pl.BlockSpec(memory_space=pltpu.HBM),
        scratch_shapes=[
            pltpu.VMEM((taps, 3, 3, channels, channels), f32),
            pltpu.VMEM((taps, 3, 3 * channels, channels), bf16),
            pltpu.VMEM((taps, 3, 3 * channels, channels), bf16),
            pltpu.VMEM((frames, rows, channels, cols), f32),
            pltpu.VMEM((frames, 2, channels, cols), f32),
            pltpu.VMEM((frames, rows + 2, channels, cols), bf16),
            pltpu.VMEM((frames, rows + 2, channels, cols), bf16),
            pltpu.VMEM((frames, 3 * channels, rows * cols), f32),
            pltpu.VMEM((frames, rows, channels, cols), f32),
            pltpu.VMEM((frames, channels * rows, cols), f32),
            pltpu.VMEM((channels, cols), f32),
            dma((taps, 3)),
            dma((frames,)),
            dma((frames,)),
            dma((frames, 2)),
            dma((frames, 2)),
            dma((frames, layers)),
            dma((frames,)),
            dma((frames,)),
        ],
        compiler_params=pltpu.CompilerParams(
            collective_id=0, has_side_effects=True, vmem_limit_bytes=48 * 1024 * 1024
        ),
        cost_estimate=pl.CostEstimate(
            flops=6 * macs, bytes_accessed=4 * conv_weight.size, transcendentals=latents.size
        ),
    )(latents.reshape(frames, channels * rows, cols), conv_weight, gain)
    return out.reshape(frames, share, rows, cols)


def solution(mesh):
    return jax.shard_map(
        local,
        mesh=mesh,
        in_specs=(
            P("groups", None, "tiles", None),
            P("section", None, None, None),
            P("section", None),
        ),
        out_specs=P("groups", "section", "tiles", None),
        check_vma=False,
    )
```

time: 193 us -> 43.5 us (0.23)
  waiting for transfers between devices: 95.1 us -> 0 us
  starting transfers between devices: 54 us -> 0 us
  Pallas kernels: 0 us -> 38.5 us
  matrix products: 19.2 us -> 0 us
  between operations: 13.4 us -> 0.01 us
  other arithmetic: 7.2 us -> 0 us
  local copies, waits for them, and re-layouts: 2.76 us -> 4.82 us
    psum x1 -> x0, waiting for transfers between devices: 75.7 us -> none  [broadcast(): return lax.psum(kept, axis)]
    ppermute x12 -> x0, starting transfers between devices: 54 us -> none  [the longest x4 29.1 us: from_behind(): return lax.ppermute(value, axis, pairs)]
    pallas_call x0 -> x1, Pallas kernels: none -> 38.5 us  [local(): pl.pallas_call(functools.partial(kernel, (frames, rows, channels, cols, l...]
    ppermute x12 -> x0, waiting for transfers between devices: 19.3 us -> none  [the longest x4 8.51 us: extended(): lax.ppermute(lax.slice_in_dim(block, 0, width, axis=dim), axis, backward)]
    dot_general x27 -> x0, matrix products: 19.2 us -> none  [convolve(): jnp.einsum('oi,tirw->torw', kernel[time_off * 9 + row_off * 3 + col_off],...]
    unnamed x1 -> x7, local copies, waits for them, and re-layouts: 1.02 us -> 4.82 us
    mul x4 -> x0, other arithmetic: 3.43 us -> none  [normalize(): return jax.nn.silu(scaled)]
    select_n x9 -> x0, other arithmetic: 2.89 us -> none  [the longest x1 1.1 us: broadcast(): jnp.where(lax.axis_index(axis) == source, value, 0).astype(value.dtype)]
  transfers between devices with their start and end apart: 13 -> 0, of which waited for: 13 -> 0; matrix products, arithmetic and copies ran while one was open for 0% -> 0% of each run, Pallas kernels for 0% -> 0%
where the time goes in v1:
time: 43.5 us; the launch traced here: 43.3 us
  Pallas kernels  38.5 us (89%)
  local copies, waits for them, and re-layouts  4.82 us (11%)
    pallas_call x1, Pallas kernels, local(): pl.pallas_call(functools.partial(kernel, (frames, rows, channels, cols, l...  38.5 us
    unnamed x7, local copies, waits for them, and re-layouts  4.82 us

profile of v1, /device:TPU:0, one launch (start us, length us, event | category | flops | bytes accessed | tf_op | source)
XLA Modules:
  0.0 43.3 jit_solution(8794408790442815508)
XLA Ops:
  0.0 0.0 copy-start
  0.0 2.5 %copy-done = f32[1,27,192,192]{3,2,1,0:T(8,128)S(1)} copy-done((f32[1,27,192,192]{3,2,1,0:T(8,128)S(1)}, f32[1,27,192,192]{3,2,1,0:T(8,128)}, u32[]{:S(2)}) %copy-start) | copy-done | bytes 3981336
  2.5 0.0 copy-start.1
  2.5 1.0 %copy-done.1 = f32[2,192,2,128]{3,2,1,0:T(2,128)S(1)} copy-done((f32[2,192,2,128]{3,2,1,0:T(2,128)S(1)}, f32[2,192,2,128]{3,2,1,0:T(2,128)}, u32[]{:S(2)}) %copy-start.1) | copy-done | bytes 393240
  3.5 0.0 copy-start.2
  3.5 0.7 %copy-done.2 = f32[1,192]{1,0:T(1,128)S(1)} copy-done((f32[1,192]{1,0:T(1,128)S(1)}, f32[1,192]{1,0:T(1,128)}, u32[]{:S(2)}) %copy-start.2) | copy-done | bytes 792
  4.2 38.5 %shard_map.37 = f32[2,96,128]{2,1,0:T(8,128)S(1)} custom-call(f32[2,384,128]{2,1,0:T(8,128)S(1)} %bitcast.3, f32[1,27,192,192]{3,2,1,0:T(8,128)S(1)} %copy-done, f32[1,192]{1,0:T(1,128)S(1)} %copy-done.2), custom_call_target="tpu_custom_call" | custom-call | flops 3057647616 | bytes 3981312 | tf_op jit(solution)/shard_map/pallas_call | solution.py:255
  42.7 0.6 %copy.5 = f32[2,48,2,128]{3,2,1,0:T(2,128)} copy(f32[2,48,2,128]{3,2,1,0:T(2,128)S(1)} %bitcast.2) | data formatting | bytes 196608
Async XLA Ops:
  0.0 2.5 %copy-start = (f32[1,27,192,192]{3,2,1,0:T(8,128)S(1)}, f32[1,27,192,192]{3,2,1,0:T(8,128)}, u32[]{:S(2)}) copy-start(f32[1,27,192,192]{3,2,1,0:T(8,128)} %weight_ref.1) | copy-start | bytes 11943940
  2.5 1.0 %copy-start.1 = (f32[2,192,2,128]{3,2,1,0:T(2,128)S(1)}, f32[2,192,2,128]{3,2,1,0:T(2,128)}, u32[]{:S(2)}) copy-start(f32[2,192,2,128]{3,2,1,0:T(2,128)} %param.3) | copy-start | bytes 1179652
  3.5 0.7 %copy-start.2 = (f32[1,192]{1,0:T(1,128)S(1)}, f32[1,192]{1,0:T(1,128)}, u32[]{:S(2)}) copy-start(f32[1,192]{1,0:T(1,128)} %gain_ref.1) | copy-start | bytes 2308

commit v2 on v1

v2 whole, which is shorter than its diff:
```python
import functools

import jax
import jax.numpy as jnp
from jax import lax
from jax.experimental import pallas as pl
from jax.experimental.pallas import tpu as pltpu
from jax.sharding import PartitionSpec as P

EPSILON = 1e-06
MESH = pl.DeviceIdType.MESH


def halves(value):
    high = value.astype(jnp.bfloat16)
    low = (value - high.astype(jnp.float32)).astype(jnp.bfloat16)
    return high, low


def kernel(
    dims,
    lat_ref, weight_ref, gain_ref, out_ref,
    lat, raw, gain_row, weights, main, halo, normed, acc, result, stage, gain_col,
    lat_sem, gain_sem, weight_sem, main_send, main_recv, edge_send, edge_recv,
    out_send, out_recv, own_sem,
):
    frames, rows, channels, cols, layers, tiles, first_tap, chunks, depth = dims
    share = channels // layers
    part = channels // chunks
    section = lax.axis_index("section")
    tile = lax.axis_index("tiles")
    last = layers - 1
    has_up = tile > 0
    has_down = tile < tiles - 1
    taps = 3 - first_tap
    even = section % 2 == 0
    direct_out = even & (section < last)
    sides = ((has_up, -1), (has_down, 1))

    def weight_copy(a, b):
        return pltpu.make_async_copy(
            weight_ref.at[0, pl.ds(9 * (a + first_tap) + 3 * b, 3)],
            raw.at[a, b],
            weight_sem.at[a, b],
        )

    lat_copy = pltpu.make_async_copy(lat_ref, lat, lat_sem)
    gain_copy = pltpu.make_async_copy(gain_ref, gain_row, gain_sem)

    @pl.when(section == 0)
    def _():
        lat_copy.start()

    gain_copy.start()
    order = [(a, b) for a in reversed(range(taps)) for b in (1, 0, 2)]
    for a, b in order:
        weight_copy(a, b).start()

    barrier = pltpu.get_barrier_semaphore()
    links = [
        (section > 0, {"section": section - 1}),
        (section < last, {"section": section + 1}),
        (section < last, {"section": last}),
    ]
    links += [(section == last, {"section": peer}) for peer in range(last)]
    for present, step in sides:
        links.append((present & even, {"tiles": tile + step}))
        links.append((present & direct_out, {"tiles": tile + step, "section": section + 1}))
        links.append(
            (present & jnp.logical_not(even), {"tiles": tile + step, "section": section - 1})
        )

    def greet(condition, target):
        @pl.when(condition)
        def _():
            pl.semaphore_signal(barrier, inc=1, device_id=target, device_id_type=MESH)

    for condition, target in links:
        greet(condition, target)

    def piece(k):
        return pl.ds(k * part, part)

    def edge_copy(f, k, side, direct):
        source = result if direct else main
        target = {"tiles": tile + sides[side][1]}
        if direct:
            target["section"] = section + 1
        return pltpu.make_async_remote_copy(
            src_ref=source.at[f, 0 if side == 0 else rows - 1, piece(k)],
            dst_ref=halo.at[f, 1 - side, piece(k)],
            send_sem=edge_send.at[f, k, side, int(direct)],
            recv_sem=edge_recv.at[f, k, 1 - side],
            device_id=target, device_id_type=MESH,
        )

    def main_copy(f, k):
        return pltpu.make_async_remote_copy(
            src_ref=result.at[f, :, piece(k)], dst_ref=main.at[f, :, piece(k)],
            send_sem=main_send.at[f, k], recv_sem=main_recv.at[f, k],
            device_id={"section": section + 1}, device_id_type=MESH,
        )

    def out_copy(f, peer):
        return pltpu.make_async_remote_copy(
            src_ref=stage.at[f, pl.ds(peer * share * rows, share * rows)],
            dst_ref=out_ref.at[f],
            send_sem=out_send.at[f, peer], recv_sem=out_recv.at[f],
            device_id={"section": peer}, device_id_type=MESH,
        )

    def own_copy(f):
        return pltpu.make_async_copy(
            stage.at[f, pl.ds(last * share * rows, share * rows)], out_ref.at[f], own_sem.at[f]
        )

    def send_edges(f, k, direct):
        for side, (present, _) in enumerate(sides):
            @pl.when(present)
            def _():
                edge_copy(f, k, side, direct).start()

    @pl.when(section == 0)
    def _():
        lat_copy.wait()
        for f in range(frames):
            for r in range(rows):
                main[f, r] = lat[f, pl.ds(r, channels, stride=rows), :]

    for side, (present, _) in enumerate(sides):
        @pl.when(jnp.logical_not(present))
        def _():
            for f in range(frames):
                halo[f, side] = jnp.zeros((channels, cols), jnp.float32)

    pl.semaphore_wait(barrier, sum(condition.astype(jnp.int32) for condition, _ in links))

    @pl.when(section == 0)
    def _():
        for f in range(frames):
            for k in range(chunks):
                send_edges(f, k, False)

    gain_copy.wait()
    diagonal = lax.broadcasted_iota(jnp.int32, (channels, channels), 0) == (
        lax.broadcasted_iota(jnp.int32, (channels, channels), 1)
    )
    column = jnp.sum(
        jnp.where(diagonal, jnp.broadcast_to(gain_row[0:1, :], (channels, channels)), 0.0),
        axis=1, keepdims=True,
    )
    gain_col[...] = jnp.broadcast_to(column, (channels, cols))

    blank = jnp.zeros((depth - channels, cols), jnp.bfloat16)
    for f in range(frames):
        for r in range(rows + 2):
            for h in range(2):
                normed[f, r, h, pl.ds(channels, depth - channels), :] = blank

    rim = jnp.zeros((channels, depth - channels), jnp.bfloat16)
    for a, b in order:
        weight_copy(a, b).wait()
        for e in range(3):
            for h, half in enumerate(halves(raw[a, b, e])):
                half = jnp.concatenate([half, rim], axis=1)
                for k in range(chunks):
                    weights[
                        h, a, pl.ds((3 * k + e) * part, part), pl.ds(b * depth, depth)
                    ] = half[k * part : (k + 1) * part]

    def normalize(values, f, place):
        meansq = jnp.mean(values * values, axis=0, keepdims=True)
        scaled = values * lax.rsqrt(meansq + EPSILON) * gain_col[...]
        for h, half in enumerate(halves(scaled / (1.0 + jnp.exp(-scaled)))):
            normed[f, place, h, pl.ds(0, channels), :] = half

    def product(f, a, offsets, first, count):
        source = f - 2 + a + first_tap
        left = [
            weights[h, a, pl.ds(first, count), pl.ds(b * depth, depth)]
            for h in (0, 1, 0) for b in offsets
        ]
        right = [
            jnp.concatenate([normed[source, r + b, h] for r in range(rows)], axis=1)
            for h in (0, 0, 1) for b in offsets
        ]
        return jnp.dot(
            jnp.concatenate(left, axis=1),
            jnp.concatenate(right, axis=0),
            preferred_element_type=jnp.float32,
        )

    lane = lax.broadcasted_iota(jnp.int32, (part, cols), 1)

    for f in range(frames):
        fresh = True
        for a in range(taps - 1):
            if f - 2 + a + first_tap >= 0:
                value = product(f, a, (0, 1, 2), 0, 3 * channels)
                acc[f] = value if fresh else acc[f] + value
                fresh = False

        @pl.when(section > 0)
        def _():
            for k in range(chunks):
                main_copy(f, k).wait_recv()

                @pl.when(even)
                def _():
                    send_edges(f, k, False)

        for r in range(rows):
            normalize(main[f, r], f, r + 1)
        value = product(f, taps - 1, (1,), 0, 3 * channels)
        acc[f] = value if fresh else acc[f] + value

        for side, (present, _) in enumerate(sides):
            @pl.when(present)
            def _():
                for k in range(chunks):
                    edge_copy(f, k, 1 - side, False).wait_recv()

        normalize(halo[f, 0], f, 0)
        normalize(halo[f, 1], f, rows + 1)
        for k in range(chunks):
            base = 3 * k * part
            value = acc[f, pl.ds(base, 3 * part), :] + product(
                f, taps - 1, (0, 2), base, 3 * part
            )
            for r in range(rows):
                span = slice(r * cols, (r + 1) * cols)
                before = pltpu.roll(value[:part, span], 1, 1)
                after = pltpu.roll(value[2 * part :, span], cols - 1, 1)
                result[f, r, piece(k)] = (
                    main[f, r, piece(k)]
                    + value[part : 2 * part, span]
                    + jnp.where(lane > 0, before, 0.0)
                    + jnp.where(lane < cols - 1, after, 0.0)
                )

            @pl.when(section < last)
            def _():
                @pl.when(even)
                def _():
                    send_edges(f, k, True)

                main_copy(f, k).start()

            @pl.when(section == last)
            def _():
                for r in range(rows):
                    stage[f, pl.ds(k * part * rows + r, part, stride=rows), :] = result[
                        f, r, piece(k)
                    ]
                for peer in range(k * layers // chunks, (k + 1) * layers // chunks):
                    if peer < last:
                        out_copy(f, peer).start()
                    else:
                        own_copy(f).start()

    for f in range(frames):
        for k in range(chunks):
            for side, (present, _) in enumerate(sides):
                @pl.when(present & even)
                def _():
                    edge_copy(f, k, side, False).wait_send()

                @pl.when(present & direct_out)
                def _():
                    edge_copy(f, k, side, True).wait_send()

            @pl.when(section < last)
            def _():
                main_copy(f, k).wait_send()

        @pl.when(section == last)
        def _():
            for peer in range(last):
                out_copy(f, peer).wait_send()
            own_copy(f).wait()

    @pl.when(section < last)
    def _():
        for f in range(frames):
            out_copy(f, 0).wait_recv()


def local(latents, conv_weight, gain):
    frames, channels, rows, cols = latents.shape
    layers = lax.axis_size("section")
    tiles = lax.axis_size("tiles")
    share = channels // layers
    first_tap = max(0, 3 - frames)
    taps = 3 - first_tap
    chunks = 2
    depth = -(-channels // 256) * 256
    f32, bf16 = jnp.float32, jnp.bfloat16
    dma = pltpu.SemaphoreType.DMA
    macs = frames * rows * cols * channels * channels * 27
    dims = (frames, rows, channels, cols, layers, tiles, first_tap, chunks, depth)
    out = pl.pallas_call(
        functools.partial(kernel, dims),
        out_shape=jax.ShapeDtypeStruct((frames, share * rows, cols), f32),
        in_specs=[pl.BlockSpec(memory_space=pltpu.HBM)] * 3,
        out_specs=pl.BlockSpec(memory_space=pltpu.HBM),
        scratch_shapes=[
            pltpu.VMEM((frames, channels * rows, cols), f32),
            pltpu.VMEM((taps, 3, 3, channels, channels), f32),
            pltpu.VMEM((1, channels), f32),
            pltpu.VMEM((2, taps, 3 * channels, 3 * depth), bf16),
            pltpu.VMEM((frames, rows, channels, cols), f32),
            pltpu.VMEM((frames, 2, channels, cols), f32),
            pltpu.VMEM((frames, rows + 2, 2, depth, cols), bf16),
            pltpu.VMEM((frames, 3 * channels, rows * cols), f32),
            pltpu.VMEM((frames, rows, channels, cols), f32),
            pltpu.VMEM((frames, channels * rows, cols), f32),
            pltpu.VMEM((channels, cols), f32),
            dma(()),
            dma(()),
            dma((taps, 3)),
            dma((frames, chunks)),
            dma((frames, chunks)),
            dma((frames, chunks, 2, 2)),
            dma((frames, chunks, 2)),
            dma((frames, layers)),
            dma((frames,)),
            dma((frames,)),
        ],
        compiler_params=pltpu.CompilerParams(
            collective_id=0, has_side_effects=True, vmem_limit_bytes=64 * 1024 * 1024
        ),
        cost_estimate=pl.CostEstimate(
            flops=6 * macs, bytes_accessed=4 * conv_weight.size, transcendentals=latents.size
        ),
    )(latents.reshape(frames, channels * rows, cols), conv_weight, gain)
    return out.reshape(frames, share, rows, cols)


def solution(mesh):
    return jax.shard_map(
        local,
        mesh=mesh,
        in_specs=(
            P("groups", None, "tiles", None),
            P("section", None, None, None),
            P("section", None),
        ),
        out_specs=P("groups", "section", "tiles", None),
        check_vma=False,
    )
```

time: 43.5 us -> 36.6 us (0.84)
  Pallas kernels: 38.5 us -> 34.9 us
  local copies, waits for them, and re-layouts: 4.82 us -> 1.54 us
    pallas_call x1, Pallas kernels: 38.5 us -> 34.9 us  [local(): pl.pallas_call(functools.partial(kernel, dims), out_shape=jax.ShapeDtypeS...]
    unnamed x7 -> x1, local copies, waits for them, and re-layouts: 4.82 us -> 1.54 us
where the time goes in v2:
time: 36.6 us; the launch traced here: 36.5 us
  Pallas kernels  34.9 us (95%)
  local copies, waits for them, and re-layouts  1.54 us (4%)
    pallas_call x1, Pallas kernels, local(): pl.pallas_call(functools.partial(kernel, dims), out_shape=jax.ShapeDtypeS...  34.9 us
    unnamed x1, local copies, waits for them, and re-layouts  1.54 us

profile of v2, /device:TPU:0, one launch (start us, length us, event | category | flops | bytes accessed | tf_op | source)
XLA Modules:
  0.0 36.5 jit_solution(7315398178327053401)
XLA Ops:
  0.0 34.9 %shard_map.37 = f32[2,96,128]{2,1,0:T(8,128)} custom-call(f32[2,384,128]{2,1,0:T(8,128)} %bitcast.3, f32[1,27,192,192]{3,2,1,0:T(8,128)} %weight_ref.1, f32[1,192]{1,0:T(1,128)} %gain_ref.1), custom_call_target="tpu_custom_call" | custom-call | flops 3057647616 | bytes 3981312 | tf_op jit(solution)/shard_map/pallas_call | solution.py:301
  34.9 1.5 %copy.5 = f32[2,48,2,128]{3,2,1,0:T(2,128)} copy(f32[2,48,2,128]{3,2,1,0:T(2,128)} %bitcast.2) | data formatting | bytes 196608

commit v3 on v2

--- a/solution.py
+++ b/solution.py
@@ -176,19 +176,27 @@
 
     def product(f, a, offsets, first, count):
         source = f - 2 + a + first_tap
-        left = [
-            weights[h, a, pl.ds(first, count), pl.ds(b * depth, depth)]
-            for h in (0, 1, 0) for b in offsets
-        ]
-        right = [
-            jnp.concatenate([normed[source, r + b, h] for r in range(rows)], axis=1)
-            for h in (0, 0, 1) for b in offsets
-        ]
-        return jnp.dot(
-            jnp.concatenate(left, axis=1),
-            jnp.concatenate(right, axis=0),
+        high, low = (
+            jnp.concatenate([weights[h, a, pl.ds(first, count), pl.ds(b * depth, depth)] for b in offsets], axis=1)
+            for h in range(2)
+        )
+
+        def windows(h):
+            return [
+                jnp.concatenate([normed[source, r + b, h] for b in offsets], axis=0)
+                for r in range(rows)
+            ]
+
+        width = rows * cols
+        wide = jnp.dot(
+            high,
+            jnp.concatenate(windows(0) + windows(1), axis=1),
             preferred_element_type=jnp.float32,
         )
+        rest = jnp.dot(
+            low, jnp.concatenate(windows(0), axis=1), preferred_element_type=jnp.float32
+        )
+        return wide[:, :width] + (wide[:, width:] + rest)
 
     lane = lax.broadcasted_iota(jnp.int32, (part, cols), 1)
 

time: 36.6 us -> 36.6 us (level)
  no operation moved by 1% of the time
where the time goes in v3:
time: 36.6 us; the launch traced here: 36.4 us
  Pallas kernels  34.9 us (95%)
  local copies, waits for them, and re-layouts  1.54 us (4%)
    pallas_call x1, Pallas kernels, local(): pl.pallas_call(functools.partial(kernel, dims), out_shape=jax.ShapeDtypeS...  34.9 us
    unnamed x1, local copies, waits for them, and re-layouts  1.54 us

profile of v3, /device:TPU:0, one launch (start us, length us, event | category | flops | bytes accessed | tf_op | source)
XLA Modules:
  0.0 36.4 jit_solution(975611521820320850)
XLA Ops:
  0.0 34.9 %shard_map.37 = f32[2,96,128]{2,1,0:T(8,128)} custom-call(f32[2,384,128]{2,1,0:T(8,128)} %bitcast.3, f32[1,27,192,192]{3,2,1,0:T(8,128)} %weight_ref.1, f32[1,192]{1,0:T(1,128)} %gain_ref.1), custom_call_target="tpu_custom_call" | custom-call | flops 3057647616 | bytes 3981312 | tf_op jit(solution)/shard_map/pallas_call | solution.py:309
  34.9 1.5 %copy.5 = f32[2,48,2,128]{3,2,1,0:T(2,128)} copy(f32[2,48,2,128]{3,2,1,0:T(2,128)} %bitcast.2) | data formatting | bytes 196608

commit v4 on v3

--- a/solution.py
+++ b/solution.py
@@ -34,7 +34,7 @@
     has_down = tile < tiles - 1
     taps = 3 - first_tap
     even = section % 2 == 0
-    direct_out = even & (section < last)
+    sends_on = section < last
     sides = ((has_up, -1), (has_down, 1))
 
     def weight_copy(a, b):
@@ -65,10 +65,8 @@
     links += [(section == last, {"section": peer}) for peer in range(last)]
     for present, step in sides:
         links.append((present & even, {"tiles": tile + step}))
-        links.append((present & direct_out, {"tiles": tile + step, "section": section + 1}))
-        links.append(
-            (present & jnp.logical_not(even), {"tiles": tile + step, "section": section - 1})
-        )
+        links.append((present & sends_on, {"tiles": tile + step, "section": section + 1}))
+        links.append((present & (section > 0), {"tiles": tile + step, "section": section - 1}))
 
     def greet(condition, target):
         @pl.when(condition)
@@ -212,10 +210,10 @@
         def _():
             for k in range(chunks):
                 main_copy(f, k).wait_recv()
-
-                @pl.when(even)
-                def _():
-                    send_edges(f, k, False)
+                if k < chunks - 1:
+                    @pl.when(even)
+                    def _():
+                        send_edges(f, k, False)
 
         for r in range(rows):
             normalize(main[f, r], f, r + 1)
@@ -248,11 +246,13 @@
 
             @pl.when(section < last)
             def _():
-                @pl.when(even)
-                def _():
+                main_copy(f, k).start()
+                if k < chunks - 1:
+                    @pl.when(even)
+                    def _():
+                        send_edges(f, k, True)
+                else:
                     send_edges(f, k, True)
-
-                main_copy(f, k).start()
 
             @pl.when(section == last)
             def _():
@@ -269,11 +269,13 @@
     for f in range(frames):
         for k in range(chunks):
             for side, (present, _) in enumerate(sides):
-                @pl.when(present & even)
+                whole = k == chunks - 1
+
+                @pl.when(present & ((section == 0) if whole else even))
                 def _():
                     edge_copy(f, k, side, False).wait_send()
 
-                @pl.when(present & direct_out)
+                @pl.when(present & (sends_on if whole else sends_on & even))
                 def _():
                     edge_copy(f, k, side, True).wait_send()
 

time: 36.6 us -> 36 us (0.984)
  Pallas kernels: 34.9 us -> 34.3 us
    pallas_call x1, Pallas kernels: 34.9 us -> 34.3 us  [local(): pl.pallas_call(functools.partial(kernel, dims), out_shape=jax.ShapeDtypeS...]
where the time goes in v4:
time: 36 us; the launch traced here: 35.9 us
  Pallas kernels  34.3 us (95%)
  local copies, waits for them, and re-layouts  1.54 us (4%)
    pallas_call x1, Pallas kernels, local(): pl.pallas_call(functools.partial(kernel, dims), out_shape=jax.ShapeDtypeS...  34.3 us
    unnamed x1, local copies, waits for them, and re-layouts  1.54 us

profile of v4, /device:TPU:0, one launch (start us, length us, event | category | flops | bytes accessed | tf_op | source)
XLA Modules:
  0.0 35.9 jit_solution(719420958804062771)
XLA Ops:
  0.0 34.3 %shard_map.37 = f32[2,96,128]{2,1,0:T(8,128)} custom-call(f32[2,384,128]{2,1,0:T(8,128)} %bitcast.3, f32[1,27,192,192]{3,2,1,0:T(8,128)} %weight_ref.1, f32[1,192]{1,0:T(1,128)} %gain_ref.1), custom_call_target="tpu_custom_call" | custom-call | flops 3057647616 | bytes 3981312 | tf_op jit(solution)/shard_map/pallas_call | solution.py:311
  34.4 1.5 %copy.5 = f32[2,48,2,128]{3,2,1,0:T(2,128)} copy(f32[2,48,2,128]{3,2,1,0:T(2,128)} %bitcast.2) | data formatting | bytes 196608

commit v5 on v4

--- a/solution.py
+++ b/solution.py
@@ -302,7 +302,7 @@
     share = channels // layers
     first_tap = max(0, 3 - frames)
     taps = 3 - first_tap
-    chunks = 2
+    chunks = 4
     depth = -(-channels // 256) * 256
     f32, bf16 = jnp.float32, jnp.bfloat16
     dma = pltpu.SemaphoreType.DMA

time: 36 us -> 36.8 us (1.022)
  Pallas kernels: 34.3 us -> 35.1 us
    pallas_call x1, Pallas kernels: 34.3 us -> 35.1 us  [local(): pl.pallas_call(functools.partial(kernel, dims), out_shape=jax.ShapeDtypeS...]
where the time goes in v5:
time: 36.8 us; the launch traced here: 36.7 us
  Pallas kernels  35.1 us (95%)
  local copies, waits for them, and re-layouts  1.54 us (4%)
    pallas_call x1, Pallas kernels, local(): pl.pallas_call(functools.partial(kernel, dims), out_shape=jax.ShapeDtypeS...  35.1 us
    unnamed x1, local copies, waits for them, and re-layouts  1.54 us

profile of v5, /device:TPU:0, one launch (start us, length us, event | category | flops | bytes accessed | tf_op | source)
XLA Modules:
  0.0 36.7 jit_solution(4607502895333493112)
XLA Ops:
  0.0 35.1 %shard_map.37 = f32[2,96,128]{2,1,0:T(8,128)} custom-call(f32[2,384,128]{2,1,0:T(8,128)} %bitcast.3, f32[1,27,192,192]{3,2,1,0:T(8,128)} %weight_ref.1, f32[1,192]{1,0:T(1,128)} %gain_ref.1), custom_call_target="tpu_custom_call" | custom-call | flops 3057647616 | bytes 3981312 | tf_op jit(solution)/shard_map/pallas_call | solution.py:311
  35.1 1.5 %copy.5 = f32[2,48,2,128]{3,2,1,0:T(2,128)} copy(f32[2,48,2,128]{3,2,1,0:T(2,128)} %bitcast.2) | data formatting | bytes 196608

commit v6 on v4

--- a/solution.py
+++ b/solution.py
@@ -217,8 +217,10 @@
 
         for r in range(rows):
             normalize(main[f, r], f, r + 1)
-        value = product(f, taps - 1, (1,), 0, 3 * channels)
-        acc[f] = value if fresh else acc[f] + value
+        split = f == frames - 1
+        if split:
+            value = product(f, taps - 1, (1,), 0, 3 * channels)
+            acc[f] = value if fresh else acc[f] + value
 
         for side, (present, _) in enumerate(sides):
             @pl.when(present)
@@ -228,11 +230,14 @@
 
         normalize(halo[f, 0], f, 0)
         normalize(halo[f, 1], f, rows + 1)
+        if not split:
+            value = product(f, taps - 1, (0, 1, 2), 0, 3 * channels)
+            acc[f] = value if fresh else acc[f] + value
         for k in range(chunks):
             base = 3 * k * part
-            value = acc[f, pl.ds(base, 3 * part), :] + product(
-                f, taps - 1, (0, 2), base, 3 * part
-            )
+            value = acc[f, pl.ds(base, 3 * part), :]
+            if split:
+                value += product(f, taps - 1, (0, 2), base, 3 * part)
             for r in range(rows):
                 span = slice(r * cols, (r + 1) * cols)
                 before = pltpu.roll(value[:part, span], 1, 1)

time: 36 us -> 37.9 us (1.053)
  Pallas kernels: 34.3 us -> 36.2 us
    pallas_call x1, Pallas kernels: 34.3 us -> 36.2 us  [local(): pl.pallas_call(functools.partial(kernel, dims), out_shape=jax.ShapeDtypeS...]
where the time goes in v6:
time: 37.9 us; the launch traced here: 37.8 us
  Pallas kernels  36.2 us (96%)
  local copies, waits for them, and re-layouts  1.54 us (4%)
    pallas_call x1, Pallas kernels, local(): pl.pallas_call(functools.partial(kernel, dims), out_shape=jax.ShapeDtypeS...  36.2 us
    unnamed x1, local copies, waits for them, and re-layouts  1.54 us

profile of v6, /device:TPU:0, one launch (start us, length us, event | category | flops | bytes accessed | tf_op | source)
XLA Modules:
  0.0 37.8 jit_solution(3639311453179028560)
XLA Ops:
  0.0 36.2 %shard_map.37 = f32[2,96,128]{2,1,0:T(8,128)} custom-call(f32[2,384,128]{2,1,0:T(8,128)} %bitcast.3, f32[1,27,192,192]{3,2,1,0:T(8,128)} %weight_ref.1, f32[1,192]{1,0:T(1,128)} %gain_ref.1), custom_call_target="tpu_custom_call" | custom-call | flops 3057647616 | bytes 3981312 | tf_op jit(solution)/shard_map/pallas_call | solution.py:316
  36.3 1.5 %copy.5 = f32[2,48,2,128]{3,2,1,0:T(2,128)} copy(f32[2,48,2,128]{3,2,1,0:T(2,128)} %bitcast.2) | data formatting | bytes 196608
